TPU v7x, 512 devices: a whole 4x4x16 slice. The times are simulated.
512 devices in a mesh: span: 8 (over x, y_hi), seq: 64 (over y_lo, z, core).
Axes of the slice: x: 4, y: 4 (y_hi: 2, y_lo: 2; y = y_hi * 2 + y_lo), z: 16, core: 2. Of those that a mesh axis runs over, the one named last changes fastest.
Arguments:
- queries: bfloat16 [8, 512, 2560], P('span', 'seq'), may hold values from -8 to 8
- keys: bfloat16 [8, 512, 2560], P('span', 'seq'), may hold values from -8 to 8
- values: bfloat16 [8, 512, 2560], P('span', 'seq'), may hold values from -6 to 6
- span_index: int32 [8], replicated, may hold values from 0 to 7, each once
Outputs:
- attended: bfloat16 [8, 512, 2560], P('span', 'seq')
Inputs may be any that keep to these rules, and one draw needn't show every extreme that they name: A permutation; group g denoises span span_index[g] and attends to itself and to the group holding the span before it.
All inputs are finite; a program needn't handle non-finite values.
Results may differ from a plain program's by a relative error of at most 0.015.
Values may be sent and summed in bfloat16 or wider, within the bound.
A program may use at most 64 MiB of HBM per device.

v0:
```python
import jax
import jax.numpy as jnp
from jax import lax
from jax.sharding import PartitionSpec as P

HEADS = 20


def fresh_state(head_count, tok_rows, head_size):
    return (
        jnp.zeros((head_count, tok_rows, head_size), jnp.float32),
        jnp.full((head_count, tok_rows), -1e30, jnp.float32),
        jnp.zeros((head_count, tok_rows), jnp.float32),
    )


def absorb(att_state, query_block, key_block, value_block, key_mask, score_scale):
    accum_part, row_max, weight_sum = att_state
    scores = (
        jnp.einsum("qhd,khd->hqk", query_block, key_block, preferred_element_type=jnp.float32)
        * score_scale
    )
    scores = jnp.where(key_mask[None, None, :], scores, -1e30)
    new_max = jnp.maximum(row_max, jnp.max(scores, axis=-1))
    weights = jnp.where(key_mask[None, None, :], jnp.exp(scores - new_max[..., None]), 0.0)
    weight_sum = jnp.sum(weights, axis=-1)
    product = jnp.einsum(
        "hqk,khd->hqd",
        weights.astype(jnp.bfloat16),
        value_block,
        preferred_element_type=jnp.float32,
    )
    accum_part = product
    return (accum_part, new_max, weight_sum)


def shards(queries, keys, values, span_index):
    tok_rows = queries.shape[1]
    feat_width = queries.shape[2]
    head_count = HEADS
    head_size = feat_width // head_count
    score_scale = head_size ** (-0.5)
    group_count = lax.axis_size("span")
    my_group = lax.axis_index("span")
    group_ids = jnp.arange(group_count, dtype=jnp.int32)
    my_span = jnp.sum(jnp.where(group_ids == my_group, span_index, 0))
    is_before = span_index == my_span - 1
    has_before = jnp.any(is_before)
    source_group = jnp.sum(jnp.where(is_before, group_ids, 0))
    own_q = queries[0].reshape(tok_rows, head_count, head_size)
    own_pair = jnp.stack([keys[0], values[0]])
    cached = lax.all_gather(own_pair[None], "span", axis=0, tiled=True)
    picked = lax.dynamic_index_in_dim(cached, source_group, 0, keepdims=False)
    own_piece = lax.all_gather(own_pair, "seq", axis=1, tiled=True)
    cache_piece = lax.all_gather(picked, "seq", axis=1, tiled=True)
    piece_rows = own_piece.shape[1]
    key_block = jnp.concatenate([own_piece[0], cache_piece[0]], 0).reshape(
        2 * piece_rows, head_count, head_size
    )
    value_block = jnp.concatenate([own_piece[1], cache_piece[1]], 0).reshape(
        2 * piece_rows, head_count, head_size
    )
    key_mask = jnp.concatenate([jnp.ones((piece_rows,), bool), jnp.full((piece_rows,), has_before)])
    accum_part, row_max, weight_sum = absorb(
        fresh_state(head_count, tok_rows, head_size),
        own_q,
        key_block,
        value_block,
        key_mask,
        score_scale,
    )
    result = (
        (accum_part / weight_sum[..., None]).transpose(1, 0, 2).reshape(1, tok_rows, feat_width)
    )
    return result.astype(jnp.bfloat16)


def solution(mesh):
    in_specs = (P("span", "seq", None), P("span", "seq", None), P("span", "seq", None), P())
    out_specs = P("span", "seq", None)
    return jax.shard_map(shards, mesh=mesh, in_specs=in_specs, out_specs=out_specs, check_vma=False)
```

profile of v0, /device:TPU:1, one launch (start us, length us, event | category | flops | bytes accessed | tf_op | source)
XLA Modules:
  0.0 356.9 jit_solution(17547577183526951520)
XLA Ops:
  6.5 0.0 copy-start
  6.5 0.0 all-gather.7.cloned.1.call-start
  6.5 1.3 fusion.37
  8.5 1.3 fusion.36
  11.1 0.8 constant_dynamic-update-slice_fusion.1
  11.9 0.8 constant_dynamic-update-slice_fusion
  12.7 31.1 %all-gather = bf16[16,8,2560]{2,1,0:T(8,128)(2,1)S(1)} all-gather(bf16[2,8,2560]{2,1,0:T(8,128)(2,1)S(1)} %constant_dynamic-update-slice_fusion), channel_id=2, replica_groups=mesh['span'=8,'seq'=64] {'span'}, dimensions={0}, use_global_device_ids=true | all-gather | bytes 737280 | tf_op jit(solution)/shard_map/all_gather | solution.py:52
  44.4 0.7 copy.22
  45.1 0.0 all-gather.7.cloned.1.call-update
  45.1 0.0 all-gather.5.cloned.1.call-start
  45.2 0.7 copy.11
  45.9 0.0 all-gather.5.cloned.1.call-update
  45.9 1.3 compare_reduce_fusion
  47.2 0.6 concatenate.19
  47.9 133.1 %all-gather.7.cloned.1.call-done = bf16[1,2,512,2560]{3,1,0,2:T(2,128)(2,1)} async-done(((bf16[1,2,8,2560]{3,1,0,2:T(2,128)(2,1)}), bf16[1,2,512,2560]{3,1,0,2:T(2,128)(2,1)}) %all-gather.7.cloned.1.call-update) | async-done | bytes 5242896 | tf_op jit(solution)/shard_map/all_gather | solution.py:55
  181.0 12.0 %fusion.42 = (bf16[1,1,512,2560]{3,1,0,2:T(2,128)(2,1)}, bf16[1,1,512,2560]{3,1,0,2:T(2,128)(2,1)}) fusion(bf16[1,2,512,2560]{3,1,0,2:T(2,128)(2,1)} %all-gather.7.cloned.1.call-done), kind=kLoop, calls=%fused_computation.35 | loop fusion | bytes 10485760 | tf_op jit(solution)/shard_map/slice | solution.py:57
  193.0 9.7 %copy.23 = bf16[1,1,512,2560]{2,3,1,0:T(8,128)(2,1)S(1)} copy(bf16[1,1,512,2560]{3,1,0,2:T(2,128)(2,1)} %get-tuple-element.7) | data formatting | bytes 5242880
  202.7 2.6 copy.16
  205.3 9.7 %copy.25 = bf16[1,1,512,2560]{2,3,1,0:T(8,128)(2,1)S(1)} copy(bf16[1,1,512,2560]{3,1,0,2:T(2,128)(2,1)} %get-tuple-element.8) | data formatting | bytes 5242880
  215.0 2.6 copy.20
  217.6 87.7 %all-gather.5.cloned.1.call-done = bf16[2,512,2560]{2,0,1:T(2,128)(2,1)} async-done(((bf16[2,8,2560]{2,0,1:T(2,128)(2,1)}), bf16[2,512,2560]{2,0,1:T(2,128)(2,1)}) %all-gather.5.cloned.1.call-update) | async-done | bytes 5242896 | tf_op jit(solution)/shard_map/all_gather | solution.py:54
  305.3 11.8 %fusion.41 = (bf16[1,512,2560]{2,0,1:T(2,128)(2,1)}, bf16[1,512,2560]{2,0,1:T(2,128)(2,1)}) fusion(bf16[2,512,2560]{2,0,1:T(2,128)(2,1)} %all-gather.5.cloned.1.call-done), kind=kLoop, calls=%fused_computation.34 | loop fusion | bytes 10485760 | tf_op jit(solution)/shard_map/slice | solution.py:57
  317.2 9.7 %copy.21 = bf16[1,512,2560]{1,2,0:T(8,128)(2,1)S(1)} copy(bf16[1,512,2560]{2,0,1:T(2,128)(2,1)} %get-tuple-element.5) | data formatting | bytes 5242880
  326.8 2.6 copy.15
  329.4 0.0 copy-done
  329.4 4.1 %fusion.43 = (f32[20,8]{1,0:T(8,128)S(1)}, f32[20,8,1024]{2,1,0:T(8,128)S(1)}) fusion(bf16[1,8,2560]{2,1,0:T(8,128)(2,1)S(1)} %copy-done, bf16[512,20,128]{2,0,1:T(8,128)(2,1)} %copy.16, bf16[512,20,128]{2,0,1:T(8,128)(2,1)} %copy.15, pred[1024]{0:T(1024)(128)(4,1)S(1)} %concatenate.19), kind=kOutput, calls=%fused_computation.36 | convolution fusion | flops 52920160 | bytes 5940864 | tf_op jit(solution)/shard_map/qhd,khd->hqk/dot_general | solution.py:20
  333.5 9.7 %copy.24 = bf16[1,512,2560]{1,2,0:T(8,128)(2,1)S(1)} copy(bf16[1,512,2560]{2,0,1:T(2,128)(2,1)} %get-tuple-element.6) | data formatting | bytes 5242880
  343.2 2.6 copy.19
  345.8 0.3 fusion.29
  346.0 4.0 %fusion.26 = bf16[1,8,2560]{2,1,0:T(8,128)(2,1)} fusion(bf16[512,20,128]{2,0,1:T(8,128)(2,1)} %copy.20, bf16[512,20,128]{2,0,1:T(8,128)(2,1)} %copy.19, f32[20,8,1024]{2,1,0:T(8,128)S(1)} %get-tuple-element.10, f32[20,8]{1,0:T(8,128)S(1)} %broadcast_maximum_fusion, pred[1024]{0:T(1024)(128)(4,1)S(1)} %concatenate.19, f32[8,20]{0,1:T(8,128)S(1)} %bitcast.28), kind=kOutput, calls=%fused_computation.14 | convolution fusion | flops 52961280 | bytes 5941504 | tf_op jit(solution)/shard_map/hqk,khd->hqd/dot_general | solution.py:27
  (3 shorter events, 0.0 us)
Async XLA Ops:
  6.5 322.9 %copy-start = (bf16[1,8,2560]{2,1,0:T(8,128)(2,1)S(1)}, bf16[1,8,2560]{2,1,0:T(8,128)(2,1)}, u32[]{:S(2)}) copy-start(bf16[1,8,2560]{2,1,0:T(8,128)(2,1)} %param.4) | copy-start | bytes 122884
  6.5 174.5 %all-gather.7.cloned.1.call-start = ((), (), s32[]{:S(2)}) async-start(), calls=%async_computation.1 | async-start | bytes 5324800 | tf_op jit(solution)/shard_map/all_gather | solution.py:55
  45.1 260.2 %all-gather.5.cloned.1.call-start = ((), (), s32[]{:S(2)}) async-start(), calls=%async_computation | async-start | bytes 5324800 | tf_op jit(solution)/shard_map/all_gather | solution.py:54
Sparse Core Ops, SparseCore 0:
  45.2 135.7 all-gather.6
  183.2 122.1 all-gather.4
where the time goes:
time: 358 us; the launch traced here: 357 us
  waiting for transfers between devices  221 us (62%)
  local copies, waits for them, and re-layouts  76.5 us (21%)
  blocking collectives  31.1 us (9%)
  between operations  16.1 us (4%)
  matrix products  8.09 us (2%)
  other arithmetic  4.16 us (1%)
    all_gather x1, waiting for transfers between devices, shards(): cache_piece = lax.all_gather(picked, 'seq', axis=1, tiled=True)  133 us
    all_gather x1, waiting for transfers between devices, shards(): own_piece = lax.all_gather(own_pair, 'seq', axis=1, tiled=True)  87.7 us
    unnamed x8, local copies, waits for them, and re-layouts  40.2 us
    all_gather x1, blocking collectives, shards(): cached = lax.all_gather(own_pair[None], 'span', axis=0, tiled=True)  31.1 us
    slice x1, local copies, waits for them, and re-layouts, shards(): cache_piece[0]  12 us
    slice x1, local copies, waits for them, and re-layouts, shards(): own_piece[0]  11.8 us
  transfers between devices with their start and end apart: 2, of which 2 were waited for; matrix products, arithmetic and copies ran while one was open for 11% of the time, Pallas kernels for 0%

commit v1 on v0

v1 whole, which is shorter than its diff:
```python
import functools

import jax
import jax.numpy as jnp
from jax import lax
from jax.experimental import pallas as pl
from jax.experimental.pallas import tpu as pltpu
from jax.sharding import PartitionSpec as P

HEADS = 20
HD = 128
GROUPS = 8
SEQ = 64
ROWS = 8
HALF = SEQ // 2
CHUNK = 128
SLOTS = CHUNK // ROWS
MESH = pl.DeviceIdType.MESH
F32 = jnp.float32
BF16 = jnp.bfloat16
SCALE = HD**-0.5


def seq_of(head):
    chip = (head * 8) // 5
    z, y = chip // 2, chip % 2
    y = (y + z // 8) % 2
    return y * HALF + z * 2


def head_of(seq):
    y, z, core = seq // HALF, (seq % HALF) // 2, seq % 2
    chip = z * 2 + (y + z // 8) % 2
    head = (chip * 5 + 7) // 8
    mine = jnp.logical_and((head * 8) // 5 == chip, core == 0)
    return jnp.minimum(head, HEADS - 1), mine


def dot(a, b, dims):
    return lax.dot_general(a, b, (dims, ((), ())), preferred_element_type=F32)


def kernel(
    span_ref, q_ref, k_ref, v_ref, out_ref,
    inbox, pack, spans, picked, own, prev, stats, acc, osend, ogot,
    in_sem, span_send, span_recv, own_send, own_recv, prev_send, prev_recv, out_send, out_recv,
):
    group = lax.axis_index("span")
    me = lax.axis_index("seq")
    head, is_head = head_of(me)

    loads = [
        pltpu.make_async_copy(ref.at[0], inbox.at[i], in_sem.at[i])
        for i, ref in enumerate((q_ref, k_ref, v_ref))
    ]
    for load in loads:
        load.start()

    def peer(step):
        other = (group + step) % GROUPS
        return other, (me + HALF * ((other + group) % 2)) % SEQ

    barrier = pltpu.get_barrier_semaphore()
    for step in range(1, GROUPS):
        pl.semaphore_signal(barrier, inc=1, device_id=peer(step), device_id_type=MESH)

    @pl.when(is_head)
    def _():
        @pl.loop(1, SEQ)
        def _(step):
            pl.semaphore_signal(barrier, inc=1, device_id=(group, (me + step) % SEQ), device_id_type=MESH)

    @pl.when(jnp.logical_not(is_head))
    def _():
        for h in range(HEADS):
            pl.semaphore_signal(barrier, inc=1, device_id=(group, seq_of(h)), device_id_type=MESH)

    for load in loads:
        load.wait()
    for h in range(HEADS):
        columns = slice(h * HD, (h + 1) * HD)
        for i in range(3):
            pack[h, i] = inbox[i, :, columns]
        for i in range(2):
            spans[group, h, i] = inbox[i + 1, :, columns]

    @pl.when(is_head)
    def _():
        pl.semaphore_wait(barrier, GROUPS - 1 + SEQ - 1)

    @pl.when(jnp.logical_not(is_head))
    def _():
        pl.semaphore_wait(barrier, GROUPS - 1 + HEADS)

    def span_copy(step):
        return pltpu.make_async_remote_copy(
            src_ref=spans.at[group],
            dst_ref=spans.at[group],
            send_sem=span_send,
            recv_sem=span_recv,
            device_id=peer(step),
            device_id_type=MESH,
        )

    def own_copy(h):
        return pltpu.make_async_remote_copy(
            src_ref=pack.at[h],
            dst_ref=own.at[me],
            send_sem=own_send,
            recv_sem=own_recv,
            device_id=(group, seq_of(h)),
            device_id_type=MESH,
        )

    def prev_copy(h):
        return pltpu.make_async_remote_copy(
            src_ref=picked.at[h],
            dst_ref=prev.at[me],
            send_sem=prev_send,
            recv_sem=prev_recv,
            device_id=(group, seq_of(h)),
            device_id_type=MESH,
        )

    for step in (1, 7, 2, 6, 3, 5, 4):
        span_copy(step).start()
    for h in range(HEADS):

        @pl.when(me != seq_of(h))
        def _(h=h):
            own_copy(h).start()

    @pl.when(is_head)
    def _():
        own[me] = pack[head]

    my_span = span_ref[group]
    source = jnp.int32(0)
    before = jnp.int32(0)
    for g in range(GROUPS):
        hit = span_ref[g] == my_span - 1
        source = jnp.where(hit, g, source)
        before = jnp.where(hit, 1, before)
    pltpu.make_async_copy(spans.at[pl.ds(0, GROUPS - 1)], spans.at[pl.ds(0, GROUPS - 1)], span_recv).wait()
    for h in range(HEADS):
        picked[h] = spans[source, h]

        @pl.when(me != seq_of(h))
        def _(h=h):
            prev_copy(h).start()

    @pl.when(is_head)
    def _():
        prev[me] = picked[head]
        whole = own.at[pl.ds(0, SEQ - 1)]
        pltpu.make_async_copy(whole, whole, own_recv).wait()
        keys = own[:, 1].reshape(SEQ * ROWS, HD)
        values = own[:, 2].reshape(SEQ * ROWS, HD)

        @pl.loop(0, SEQ // SLOTS)
        def _(c):
            rows = pl.ds(pl.multiple_of(c * CHUNK, CHUNK), CHUNK)
            queries = own[pl.ds(c * SLOTS, SLOTS), 0].reshape(CHUNK, HD)
            scores = dot(queries, keys, ((1,), (1,)))
            top = jnp.max(scores, axis=1, keepdims=True)
            weights = jnp.exp((scores - top) * SCALE)
            stats[0, rows] = jnp.broadcast_to(top, (CHUNK, HD))
            stats[1, rows] = jnp.broadcast_to(jnp.sum(weights, axis=1, keepdims=True), (CHUNK, HD))
            acc[rows] = dot(weights.astype(BF16), values, ((1,), (0,)))

        whole = prev.at[pl.ds(0, SEQ - 1)]
        pltpu.make_async_copy(whole, whole, prev_recv).wait()
        keys2 = prev[:, 0].reshape(SEQ * ROWS, HD)
        values2 = prev[:, 1].reshape(SEQ * ROWS, HD)

        @pl.loop(0, SEQ // SLOTS)
        def _(c):
            rows = pl.ds(pl.multiple_of(c * CHUNK, CHUNK), CHUNK)
            queries = own[pl.ds(c * SLOTS, SLOTS), 0].reshape(CHUNK, HD)
            scores = dot(queries, keys2, ((1,), (1,)))
            scores = jnp.where(before > 0, scores, -1e30)
            old = stats[0, rows][:, :1]
            top = jnp.maximum(old, jnp.max(scores, axis=1, keepdims=True))
            weights = jnp.exp((scores - top) * SCALE)
            fade = jnp.exp((old - top) * SCALE)
            total = stats[1, rows][:, :1] * fade + jnp.sum(weights, axis=1, keepdims=True)
            result = acc[rows] * fade + dot(weights.astype(BF16), values2, ((1,), (0,)))
            result = (result / total).reshape(SLOTS, ROWS, HD)
            osend[pl.ds(c * SLOTS, SLOTS)] = result.astype(BF16)
            for i in range(SLOTS):
                slot = c * SLOTS + i

                @pl.when(slot != me)
                def _():
                    pltpu.make_async_remote_copy(
                        src_ref=osend.at[slot],
                        dst_ref=ogot.at[head],
                        send_sem=out_send,
                        recv_sem=out_recv,
                        device_id=(group, slot),
                        device_id_type=MESH,
                    ).start()

        ogot[head] = osend[me]

    @pl.when(is_head)
    def _():
        whole = ogot.at[pl.ds(0, HEADS - 1)]
        pltpu.make_async_copy(whole, whole, out_recv).wait()

    @pl.when(jnp.logical_not(is_head))
    def _():
        pltpu.make_async_copy(ogot, ogot, out_recv).wait()

    for h in range(HEADS):
        out_ref[0, :, h * HD : (h + 1) * HD] = ogot[h]

    pltpu.make_async_copy(spans.at[pl.ds(0, GROUPS - 1)], spans.at[pl.ds(0, GROUPS - 1)], span_send).wait()

    @pl.when(is_head)
    def _():
        pltpu.make_async_copy(pack.at[pl.ds(0, HEADS - 1)], pack.at[pl.ds(0, HEADS - 1)], own_send).wait()
        pltpu.make_async_copy(picked.at[pl.ds(0, HEADS - 1)], picked.at[pl.ds(0, HEADS - 1)], prev_send).wait()
        pltpu.make_async_copy(osend.at[pl.ds(0, SEQ - 1)], osend.at[pl.ds(0, SEQ - 1)], out_send).wait()

    @pl.when(jnp.logical_not(is_head))
    def _():
        pltpu.make_async_copy(pack, pack, own_send).wait()
        pltpu.make_async_copy(picked, picked, prev_send).wait()


def solution(mesh):
    def shards(queries, keys, values, span_index):
        return pl.pallas_call(
            kernel,
            out_shape=jax.ShapeDtypeStruct((1, ROWS, HEADS * HD), BF16),
            in_specs=[pl.BlockSpec(memory_space=pltpu.SMEM)] + [pl.BlockSpec(memory_space=pl.ANY)] * 3,
            out_specs=pl.BlockSpec(memory_space=pltpu.VMEM),
            scratch_shapes=[
                pltpu.VMEM((3, ROWS, HEADS * HD), BF16),
                pltpu.VMEM((HEADS, 3, ROWS, HD), BF16),
                pltpu.VMEM((GROUPS, HEADS, 2, ROWS, HD), BF16),
                pltpu.VMEM((HEADS, 2, ROWS, HD), BF16),
                pltpu.VMEM((SEQ, 3, ROWS, HD), BF16),
                pltpu.VMEM((SEQ, 2, ROWS, HD), BF16),
                pltpu.VMEM((2, SEQ * ROWS, HD), F32),
                pltpu.VMEM((SEQ * ROWS, HD), F32),
                pltpu.VMEM((SEQ, ROWS, HD), BF16),
                pltpu.VMEM((HEADS, ROWS, HD), BF16),
                pltpu.SemaphoreType.DMA((3,)),
            ]
            + [pltpu.SemaphoreType.DMA] * 8,
            compiler_params=pltpu.CompilerParams(
                collective_id=0, has_side_effects=True, vmem_limit_bytes=32 * 1024 * 1024
            ),
        )(span_index, queries, keys, values)

    in_specs = (P("span", "seq", None), P("span", "seq", None), P("span", "seq", None), P())
    return jax.shard_map(shards, mesh=mesh, in_specs=in_specs, out_specs=P("span", "seq", None), check_vma=False)
```

time: 358 us -> 49.7 us (0.14)
  waiting for transfers between devices: 221 us -> 0 us
  local copies, waits for them, and re-layouts: 76.5 us -> 3.61 us
  Pallas kernels: 0 us -> 45.8 us
  blocking collectives: 31.1 us -> 0 us
  between operations: 16.1 us -> 0.01 us
  matrix products: 8.09 us -> 0 us
  other arithmetic: 4.16 us -> 0 us
    all_gather x2 -> x0, waiting for transfers between devices: 221 us -> none  [the longest x1 133 us: shards(): cache_piece = lax.all_gather(picked, 'seq', axis=1, tiled=True)]
    pallas_call x0 -> x1, Pallas kernels: none -> 45.8 us  [shards(): pl.pallas_call(kernel, out_shape=jax.ShapeDtypeStruct((1, ROWS, HEADS * H...]
    unnamed x8 -> x9, local copies, waits for them, and re-layouts: 40.2 us -> 3.61 us
    all_gather x1 -> x0, blocking collectives: 31.1 us -> none  [shards(): cached = lax.all_gather(own_pair[None], 'span', axis=0, tiled=True)]
    slice x2 -> x0, local copies, waits for them, and re-layouts: 23.8 us -> none  [the longest x1 12 us: shards(): cache_piece[0]]
    concatenate x5 -> x0, local copies, waits for them, and re-layouts: 11 us -> none  [the longest x2 5.18 us: shards(): jnp.concatenate([own_piece[1], cache_piece[1]], 0)]
    dot_general x2 -> x0, matrix products: 8.09 us -> none  [the longest x1 4.07 us: absorb(): jnp.einsum('qhd,khd->hqk', query_block, key_block, preferred_element_type...]
  transfers between devices with their start and end apart: 2 -> 0, of which waited for: 2 -> 0; matrix products, arithmetic and copies ran while one was open for 11% -> 0% of each run, Pallas kernels for 0% -> 0%
where the time goes in v1:
time: 49.7 us; the launch traced here: 49.4 us
  Pallas kernels  45.8 us (92%)
  local copies, waits for them, and re-layouts  3.61 us (7%)
    pallas_call x1, Pallas kernels, shards(): pl.pallas_call(kernel, out_shape=jax.ShapeDtypeStruct((1, ROWS, HEADS * H...  45.8 us
    unnamed x9, local copies, waits for them, and re-layouts  3.61 us

profile of v1, /device:TPU:1, one launch (start us, length us, event | category | flops | bytes accessed | tf_op | source)
XLA Modules:
  0.0 49.4 jit_solution(13525790005183463121)
XLA Ops:
  0.0 0.0 copy-start
  0.0 0.8 %copy-done = bf16[1,8,2560]{2,1,0:T(8,128)(2,1)S(1)} copy-done((bf16[1,8,2560]{2,1,0:T(8,128)(2,1)S(1)}, bf16[1,8,2560]{2,1,0:T(8,128)(2,1)}, u32[]{:S(2)}) %copy-start) | copy-done | bytes 40984
  0.8 0.0 copy-start.1
  0.8 0.8 %copy-done.1 = bf16[1,8,2560]{2,1,0:T(8,128)(2,1)S(1)} copy-done((bf16[1,8,2560]{2,1,0:T(8,128)(2,1)S(1)}, bf16[1,8,2560]{2,1,0:T(8,128)(2,1)}, u32[]{:S(2)}) %copy-start.1) | copy-done | bytes 40984
  1.6 0.0 copy-start.2
  1.6 0.8 %copy-done.2 = bf16[1,8,2560]{2,1,0:T(8,128)(2,1)S(1)} copy-done((bf16[1,8,2560]{2,1,0:T(8,128)(2,1)S(1)}, bf16[1,8,2560]{2,1,0:T(8,128)(2,1)}, u32[]{:S(2)}) %copy-start.2) | copy-done | bytes 40984
  2.3 0.0 copy-start.3
  2.3 0.7 %copy-done.3 = s32[8]{0:T(128)S(1)} copy-done((s32[8]{0:T(128)S(1)}, s32[8]{0:T(128)}, u32[]{:S(2)}) %copy-start.3) | copy-done | bytes 56
  3.0 45.8 %shard_map.46 = bf16[1,8,2560]{2,1,0:T(8,128)(2,1)S(1)} custom-call(s32[8]{0:T(128)S(1)} %copy-done.3, bf16[1,8,2560]{2,1,0:T(8,128)(2,1)S(1)} %copy-done, bf16[1,8,2560]{2,1,0:T(8,128)(2,1)S(1)} %copy-done.1, bf16[1,8,2560]{2,1,0:T(8,128)(2,1)S(1)} %copy-done.2), custom_call_target="tpu_custom_call" | custom-call | tf_op jit(solution)/shard_map/pallas_call | solution.py:234
  48.8 0.6 %copy.6 = bf16[1,8,2560]{2,1,0:T(8,128)(2,1)} copy(bf16[1,8,2560]{2,1,0:T(8,128)(2,1)S(1)} %shard_map.46) | data formatting | bytes 81920
Async XLA Ops:
  0.0 0.8 %copy-start = (bf16[1,8,2560]{2,1,0:T(8,128)(2,1)S(1)}, bf16[1,8,2560]{2,1,0:T(8,128)(2,1)}, u32[]{:S(2)}) copy-start(bf16[1,8,2560]{2,1,0:T(8,128)(2,1)} %q_ref.1) | copy-start | bytes 122884
  0.8 0.8 %copy-start.1 = (bf16[1,8,2560]{2,1,0:T(8,128)(2,1)S(1)}, bf16[1,8,2560]{2,1,0:T(8,128)(2,1)}, u32[]{:S(2)}) copy-start(bf16[1,8,2560]{2,1,0:T(8,128)(2,1)} %k_ref.1) | copy-start | bytes 122884
  1.6 0.8 %copy-start.2 = (bf16[1,8,2560]{2,1,0:T(8,128)(2,1)S(1)}, bf16[1,8,2560]{2,1,0:T(8,128)(2,1)}, u32[]{:S(2)}) copy-start(bf16[1,8,2560]{2,1,0:T(8,128)(2,1)} %v_ref.1) | copy-start | bytes 122884
  2.3 0.7 %copy-start.3 = (s32[8]{0:T(128)S(1)}, s32[8]{0:T(128)}, u32[]{:S(2)}) copy-start(s32[8]{0:T(128)} %span_ref.1) | copy-start | bytes 100

commit v2 on v1

v2 whole, which is shorter than its diff:
```python
import functools

import jax
import jax.numpy as jnp
from jax import lax
from jax.experimental import pallas as pl
from jax.experimental.pallas import tpu as pltpu
from jax.sharding import PartitionSpec as P

HEADS = 20
HD = 128
GROUPS = 8
SEQ = 64
ROWS = 8
HALF = SEQ // 2
ZS = HALF // 2
CHUNK = 128
SLOTS = CHUNK // ROWS
MESH = pl.DeviceIdType.MESH
F32 = jnp.float32
BF16 = jnp.bfloat16
SCALE = HD**-0.5


HEAD_Z = (0, 1, 3, 4, 6, 8, 9, 11, 12, 14)
HEAD_SEQ = tuple(y * HALF + z * 2 for z in HEAD_Z for y in range(2))


def seq_of(head):
    if isinstance(head, int):
        return HEAD_SEQ[head]
    seq = jnp.int32(HEAD_SEQ[0])
    for h in range(1, HEADS):
        seq = jnp.where(head == h, HEAD_SEQ[h], seq)
    return seq


def head_of(seq):
    head = jnp.int32(0)
    mine = seq == HEAD_SEQ[0]
    for h in range(1, HEADS):
        head = jnp.where(seq == HEAD_SEQ[h], h, head)
        mine = jnp.logical_or(mine, seq == HEAD_SEQ[h])
    return head, mine


def part_of(head):
    return jnp.where(head < 2 * GROUPS, head // 2, 2 * (head - 2 * GROUPS))


def part_heads(part):
    return 2 * part, 2 * part + 1, 2 * GROUPS + part // 2


def send(kind, source, target, sems, device):
    pltpu.make_async_remote_copy(
        src_ref=source, dst_ref=target, send_sem=sems[0], recv_sem=sems[1], device_id=device, device_id_type=MESH
    ).start()


def wait(kind, ref, sem):
    pltpu.make_async_copy(ref, ref, sem).wait()


def dot(a, b, dims):
    return lax.dot_general(a, b, (dims, ((), ())), preferred_element_type=F32)


def kernel(
    span_ref, q_ref, k_ref, v_ref, out_ref,
    span, inbox, pack, parts, inter, picked, own, prev, stats, acc, osend, ogot,
    in_sem, span_sem, part_send, part_recv, own_send, own_recv, prev_send, prev_recv, out_send, out_recv,
):
    group = lax.axis_index("span")
    me = lax.axis_index("seq")
    core = me % 2
    head, is_head = head_of(me)
    z = (me % HALF) // 2
    part = (group + GROUPS - z % GROUPS) % GROUPS
    third = part % 2 == core
    to_self = jnp.logical_and(is_head, (part_of(head) + z) % GROUPS == group)

    def peer(step):
        other = (group + step) % GROUPS
        return other, (me + HALF * ((other + group) % 2)) % SEQ

    barrier = pltpu.get_barrier_semaphore()

    def greet(device):
        pl.semaphore_signal(barrier, inc=1, device_id=device, device_id_type=MESH)

    @pl.when(is_head)
    def _():
        for k in sorted(range(ZS), key=lambda k: -min(k, ZS - k)):
            for y in range(2):
                for c in range(2):
                    far = (z + k) % ZS
                    sender = y * HALF + 2 * far + c
                    via = (part_of(head) + jnp.where(head < 2 * GROUPS, 0, c) + far) % GROUPS
                    if k:
                        greet((group, sender))
                        greet((via, sender))
                    else:

                        @pl.when(sender != me)
                        def _():
                            greet((group, sender))

                        @pl.when(jnp.logical_or(via != group, sender != me))
                        def _():
                            greet((via, sender))

    @pl.when(jnp.logical_not(is_head))
    def _():
        for h in range(HEADS):
            greet((group, seq_of(h)))

    for step in range(1, GROUPS):
        greet(peer(step))

    loads = [pltpu.make_async_copy(span_ref, span, span_sem)] + [
        pltpu.make_async_copy(ref.at[0], inbox.at[i], in_sem.at[i])
        for i, ref in enumerate((q_ref, k_ref, v_ref))
    ]
    for load in loads:
        load.start()

    for load in loads:
        load.wait()
    for h in range(HEADS):
        columns = slice(h * HD, (h + 1) * HD)
        for i in range(3):
            pack[h, i] = inbox[i, :, columns]
    for p in range(GROUPS):
        for i, h in enumerate(part_heads(p)):
            for j in range(2):
                parts[p, i, j] = inbox[j + 1, :, h * HD : (h + 1) * HD]
    inter[group] = parts[part]

    spans = [span[g] for g in range(GROUPS)]
    sources = []
    for g in range(GROUPS):
        source = jnp.int32(0)
        for p in range(GROUPS):
            source = jnp.where(spans[p] == spans[g] - 1, p, source)
        sources.append(source)
    my_span = span[group]
    before = jnp.int32(0)
    for g in range(GROUPS):
        before = jnp.where(spans[g] == my_span - 1, 1, before)

    targets = [seq_of(h) for h in part_heads(part)]
    sent = 2 * GROUPS + jnp.where(third, GROUPS, 0) - jnp.where(to_self, 1, 0)
    greeted = GROUPS - 1 + jnp.where(is_head, SEQ - 1, HEADS) + sent
    pl.semaphore_wait(barrier, greeted)

    for step in (4, 3, 5, 2, 6, 1, 7):
        send("part", parts.at[(part + step) % GROUPS], inter.at[group], (part_send, part_recv), peer(step))
    for h in range(HEADS):

        @pl.when(me != seq_of(h))
        def _(h=h):
            send("own", pack.at[h], own.at[me], (own_send, own_recv), (group, seq_of(h)))

    @pl.when(is_head)
    def _():
        own[me] = pack[head]

    others = inter.at[pl.ds(0, GROUPS - 1)]
    wait("part", others, part_recv)

    def pass_on(g, i):
        target = targets[i]

        @pl.when(jnp.logical_or(group != g, me != target))
        def _():
            send("prev", picked.at[g, i], prev.at[me], (prev_send, prev_recv), (g, target))

        @pl.when(jnp.logical_and(group == g, me == target))
        def _():
            prev[me] = picked[g, i]

    for g in range(GROUPS):
        picked[g] = inter[sources[g]]
        for i in range(2):
            pass_on(g, i)

    @pl.when(third)
    def _():
        for g in range(GROUPS):
            pass_on(g, 2)

    @pl.when(is_head)
    def _():
        whole = own.at[pl.ds(0, SEQ - 1)]
        wait("own", whole, own_recv)
        keys = own[:, 1].reshape(SEQ * ROWS, HD)
        values = own[:, 2].reshape(SEQ * ROWS, HD)

        for c in (0, 2, 1, 3):
            rows = pl.ds(c * CHUNK, CHUNK)
            queries = own[pl.ds(c * SLOTS, SLOTS), 0].reshape(CHUNK, HD)
            scores = dot(queries, keys, ((1,), (1,)))
            top = jnp.max(scores, axis=1, keepdims=True)
            weights = jnp.exp((scores - top) * SCALE)
            stats[0, rows] = jnp.broadcast_to(top, (CHUNK, HD))
            stats[1, rows] = jnp.broadcast_to(jnp.sum(weights, axis=1, keepdims=True), (CHUNK, HD))
            acc[rows] = dot(weights.astype(BF16), values, ((1,), (0,)))

        @pl.when(to_self)
        def _():
            others = prev.at[pl.ds(0, SEQ - 1)]
            wait("prev", others, prev_recv)

        @pl.when(jnp.logical_not(to_self))
        def _():
            wait("prev", prev, prev_recv)

        keys2 = prev[:, 0].reshape(SEQ * ROWS, HD)
        values2 = prev[:, 1].reshape(SEQ * ROWS, HD)

        for c in (0, 2, 1, 3):
            rows = pl.ds(c * CHUNK, CHUNK)
            queries = own[pl.ds(c * SLOTS, SLOTS), 0].reshape(CHUNK, HD)
            scores = dot(queries, keys2, ((1,), (1,)))
            scores = jnp.where(before > 0, scores, -1e30)
            old = stats[0, rows][:, :1]
            top = jnp.maximum(old, jnp.max(scores, axis=1, keepdims=True))
            weights = jnp.exp((scores - top) * SCALE)
            fade = jnp.exp((old - top) * SCALE)
            total = stats[1, rows][:, :1] * fade + jnp.sum(weights, axis=1, keepdims=True)
            result = acc[rows] * fade + dot(weights.astype(BF16), values2, ((1,), (0,)))
            result = (result / total).reshape(SLOTS, ROWS, HD)
            osend[pl.ds(c * SLOTS, SLOTS)] = result.astype(BF16)
            for i in range(SLOTS):
                slot = c * SLOTS + i

                @pl.when(slot != me)
                def _(slot=slot):
                    send("out", osend.at[slot], ogot.at[head], (out_send, out_recv), (group, slot))

        ogot[head] = osend[me]

    @pl.when(is_head)
    def _():
        whole = ogot.at[pl.ds(0, HEADS - 1)]
        wait("out", whole, out_recv)

    @pl.when(jnp.logical_not(is_head))
    def _():
        wait("out", ogot, out_recv)

    for h in range(HEADS):
        out_ref[0, :, h * HD : (h + 1) * HD] = ogot[h]

    wait("part", others, part_send)

    @pl.when(is_head)
    def _():
        wait("own", pack.at[pl.ds(0, HEADS - 1)], own_send)
        wait("out", osend.at[pl.ds(0, SEQ - 1)], out_send)

    @pl.when(jnp.logical_not(is_head))
    def _():
        wait("own", pack, own_send)

    for count in (2 * GROUPS - 1, 2 * GROUPS, 3 * GROUPS - 1, 3 * GROUPS):

        @pl.when(sent == count)
        def _(count=count):
            left = prev.at[pl.ds(0, count)]
            wait("prev", left, prev_send)


def solution(mesh):
    def shards(queries, keys, values, span_index):
        return pl.pallas_call(
            kernel,
            out_shape=pltpu.VMEM((1, ROWS, HEADS * HD), BF16),
            in_specs=[pl.BlockSpec(memory_space=pl.ANY)] * 4,
            out_specs=pl.BlockSpec(memory_space=pltpu.VMEM),
            scratch_shapes=[
                pltpu.SMEM((GROUPS,), jnp.int32),
                pltpu.VMEM((3, ROWS, HEADS * HD), BF16),
                pltpu.VMEM((HEADS, 3, ROWS, HD), BF16),
                pltpu.VMEM((GROUPS, 3, 2, ROWS, HD), BF16),
                pltpu.VMEM((GROUPS, 3, 2, ROWS, HD), BF16),
                pltpu.VMEM((GROUPS, 3, 2, ROWS, HD), BF16),
                pltpu.VMEM((SEQ, 3, ROWS, HD), BF16),
                pltpu.VMEM((SEQ, 2, ROWS, HD), BF16),
                pltpu.VMEM((2, SEQ * ROWS, HD), F32),
                pltpu.VMEM((SEQ * ROWS, HD), F32),
                pltpu.VMEM((SEQ, ROWS, HD), BF16),
                pltpu.VMEM((HEADS, ROWS, HD), BF16),
                pltpu.SemaphoreType.DMA((3,)),
            ]
            + [pltpu.SemaphoreType.DMA] * 9,
            compiler_params=pltpu.CompilerParams(
                collective_id=0, has_side_effects=True, vmem_limit_bytes=60 * 1024 * 1024
            ),
        )(span_index, queries, keys, values)

    in_specs = (P("span", "seq", None), P("span", "seq", None), P("span", "seq", None), P())
    return jax.shard_map(shards, mesh=mesh, in_specs=in_specs, out_specs=P("span", "seq", None), check_vma=False)
```

time: 49.7 us -> 43.4 us (0.87)
  Pallas kernels: 45.8 us -> 42.6 us
  local copies, waits for them, and re-layouts: 3.61 us -> 0.62 us
    pallas_call x1, Pallas kernels: 45.8 us -> 42.6 us  [shards(): pl.pallas_call(kernel, out_shape=pltpu.VMEM((1, ROWS, HEADS * HD), BF16),...]
    unnamed x9 -> x1, local copies, waits for them, and re-layouts: 3.61 us -> 0.62 us
where the time goes in v2:
time: 43.4 us; the launch traced here: 43.3 us
  Pallas kernels  42.6 us (98%)
  local copies, waits for them, and re-layouts  0.62 us (1%)
    pallas_call x1, Pallas kernels, shards(): pl.pallas_call(kernel, out_shape=pltpu.VMEM((1, ROWS, HEADS * HD), BF16),...  42.6 us

profile of v2, /device:TPU:1, one launch (start us, length us, event | category | flops | bytes accessed | tf_op | source)
XLA Modules:
  0.0 43.3 jit_solution(2266649680062539397)
XLA Ops:
  0.0 42.6 %shard_map.46 = bf16[1,8,2560]{2,1,0:T(8,128)(2,1)S(1)} custom-call(s32[8]{0:T(128)} %span_ref.1, bf16[1,8,2560]{2,1,0:T(8,128)(2,1)} %q_ref.1, bf16[1,8,2560]{2,1,0:T(8,128)(2,1)} %k_ref.1, bf16[1,8,2560]{2,1,0:T(8,128)(2,1)} %v_ref.1), custom_call_target="tpu_custom_call" | custom-call | tf_op jit(solution)/shard_map/pallas_call | solution.py:277
  42.6 0.6 %copy.6 = bf16[1,8,2560]{2,1,0:T(8,128)(2,1)} copy(bf16[1,8,2560]{2,1,0:T(8,128)(2,1)S(1)} %shard_map.46) | data formatting | bytes 81920

commit v3 on v2

--- a/solution.py
+++ b/solution.py
@@ -22,7 +22,7 @@
 SCALE = HD**-0.5
 
 
-HEAD_Z = (0, 1, 3, 4, 6, 8, 9, 11, 12, 14)
+HEAD_Z = (3, 4, 6, 8, 9, 11, 12, 14, 0, 1)
 HEAD_SEQ = tuple(y * HALF + z * 2 for z in HEAD_Z for y in range(2))
 
 
@@ -69,7 +69,7 @@
 def kernel(
     span_ref, q_ref, k_ref, v_ref, out_ref,
     span, inbox, pack, parts, inter, picked, own, prev, stats, acc, osend, ogot,
-    in_sem, span_sem, part_send, part_recv, own_send, own_recv, prev_send, prev_recv, out_send, out_recv,
+    in_sem, span_sem, part_send, part_recv, own_send, own_recv, prev_send, prev_recv, out_send, out_recv, go,
 ):
     group = lax.axis_index("span")
     me = lax.axis_index("seq")
@@ -94,21 +94,17 @@
         for k in sorted(range(ZS), key=lambda k: -min(k, ZS - k)):
             for y in range(2):
                 for c in range(2):
-                    far = (z + k) % ZS
-                    sender = y * HALF + 2 * far + c
-                    via = (part_of(head) + jnp.where(head < 2 * GROUPS, 0, c) + far) % GROUPS
+                    sender = y * HALF + 2 * ((z + k) % ZS) + c
                     if k:
                         greet((group, sender))
-                        greet((via, sender))
                     else:
 
                         @pl.when(sender != me)
                         def _():
                             greet((group, sender))
 
-                        @pl.when(jnp.logical_or(via != group, sender != me))
-                        def _():
-                            greet((via, sender))
+        for step in range(1, GROUPS, 2):
+            greet(((group + step) % GROUPS, me))
 
     @pl.when(jnp.logical_not(is_head))
     def _():
@@ -139,10 +135,11 @@
 
     spans = [span[g] for g in range(GROUPS)]
     sources = []
-    for g in range(GROUPS):
+    for step in range(GROUPS):
+        wanted = span[(group + step) % GROUPS] - 1
         source = jnp.int32(0)
         for p in range(GROUPS):
-            source = jnp.where(spans[p] == spans[g] - 1, p, source)
+            source = jnp.where(spans[p] == wanted, p, source)
         sources.append(source)
     my_span = span[group]
     before = jnp.int32(0)
@@ -151,11 +148,23 @@
 
     targets = [seq_of(h) for h in part_heads(part)]
     sent = 2 * GROUPS + jnp.where(third, GROUPS, 0) - jnp.where(to_self, 1, 0)
-    greeted = GROUPS - 1 + jnp.where(is_head, SEQ - 1, HEADS) + sent
+    greeted = GROUPS - 1 + jnp.where(is_head, SEQ - 1 + GROUPS // 2, HEADS)
     pl.semaphore_wait(barrier, greeted)
 
     for step in (4, 3, 5, 2, 6, 1, 7):
         send("part", parts.at[(part + step) % GROUPS], inter.at[group], (part_send, part_recv), peer(step))
+    @pl.when(is_head)
+    def _():
+        for c in range(2):
+            low = (group + 2 * GROUPS - part_of(head) - jnp.where(head < 2 * GROUPS, 0, c)) % GROUPS
+            for far in (low, low + GROUPS):
+                for y in range(2):
+                    passer = y * HALF + 2 * far + c
+
+                    @pl.when(passer != me)
+                    def _():
+                        pl.semaphore_signal(go, inc=1, device_id=(group, passer), device_id_type=MESH)
+
     for h in range(HEADS):
 
         @pl.when(me != seq_of(h))
@@ -169,26 +178,32 @@
     others = inter.at[pl.ds(0, GROUPS - 1)]
     wait("part", others, part_recv)
 
-    def pass_on(g, i):
-        target = targets[i]
-
-        @pl.when(jnp.logical_or(group != g, me != target))
-        def _():
-            send("prev", picked.at[g, i], prev.at[me], (prev_send, prev_recv), (g, target))
-
-        @pl.when(jnp.logical_and(group == g, me == target))
-        def _():
-            prev[me] = picked[g, i]
-
-    for g in range(GROUPS):
-        picked[g] = inter[sources[g]]
+    pl.semaphore_wait(go, 2 + jnp.where(third, 1, 0) - jnp.where(to_self, 1, 0))
+
+    def pass_on(step, i):
+        def copy():
+            device = ((group + step) % GROUPS, targets[i])
+            send("prev", picked.at[step, i], prev.at[me], (prev_send, prev_recv), device)
+
+        if step:
+            copy()
+        else:
+            pl.when(me != targets[i])(copy)
+
+            @pl.when(me == targets[i])
+            def _():
+                prev[me] = picked[step, i]
+
+    order = (5, 3, 4, 7, 1, 6, 2, 0)
+    for step in order:
+        picked[step] = inter[sources[step]]
         for i in range(2):
-            pass_on(g, i)
+            pass_on(step, i)
 
     @pl.when(third)
     def _():
-        for g in range(GROUPS):
-            pass_on(g, 2)
+        for step in order:
+            pass_on(step, 2)
 
     @pl.when(is_head)
     def _():
@@ -197,9 +212,15 @@
         keys = own[:, 1].reshape(SEQ * ROWS, HD)
         values = own[:, 2].reshape(SEQ * ROWS, HD)
 
-        for c in (0, 2, 1, 3):
+        def slots_of(c):
+            return [pl.ds(y * HALF + c * SLOTS // 2, SLOTS // 2) for y in range(2)]
+
+        def queries_of(c):
+            return jnp.concatenate([own[slots, 0].reshape(CHUNK // 2, HD) for slots in slots_of(c)], 0)
+
+        for c in range(SEQ // SLOTS):
             rows = pl.ds(c * CHUNK, CHUNK)
-            queries = own[pl.ds(c * SLOTS, SLOTS), 0].reshape(CHUNK, HD)
+            queries = queries_of(c)
             scores = dot(queries, keys, ((1,), (1,)))
             top = jnp.max(scores, axis=1, keepdims=True)
             weights = jnp.exp((scores - top) * SCALE)
@@ -219,9 +240,9 @@
         keys2 = prev[:, 0].reshape(SEQ * ROWS, HD)
         values2 = prev[:, 1].reshape(SEQ * ROWS, HD)
 
-        for c in (0, 2, 1, 3):
+        for c in range(SEQ // SLOTS):
             rows = pl.ds(c * CHUNK, CHUNK)
-            queries = own[pl.ds(c * SLOTS, SLOTS), 0].reshape(CHUNK, HD)
+            queries = queries_of(c)
             scores = dot(queries, keys2, ((1,), (1,)))
             scores = jnp.where(before > 0, scores, -1e30)
             old = stats[0, rows][:, :1]
@@ -230,10 +251,11 @@
             fade = jnp.exp((old - top) * SCALE)
             total = stats[1, rows][:, :1] * fade + jnp.sum(weights, axis=1, keepdims=True)
             result = acc[rows] * fade + dot(weights.astype(BF16), values2, ((1,), (0,)))
-            result = (result / total).reshape(SLOTS, ROWS, HD)
-            osend[pl.ds(c * SLOTS, SLOTS)] = result.astype(BF16)
+            result = (result / total).reshape(2, SLOTS // 2, ROWS, HD).astype(BF16)
+            for y, slots in enumerate(slots_of(c)):
+                osend[slots] = result[y]
             for i in range(SLOTS):
-                slot = c * SLOTS + i
+                slot = (i % 2) * HALF + c * SLOTS // 2 + i // 2
 
                 @pl.when(slot != me)
                 def _(slot=slot):
@@ -294,7 +316,8 @@
                 pltpu.VMEM((HEADS, ROWS, HD), BF16),
                 pltpu.SemaphoreType.DMA((3,)),
             ]
-            + [pltpu.SemaphoreType.DMA] * 9,
+            + [pltpu.SemaphoreType.DMA] * 9
+            + [pltpu.SemaphoreType.REGULAR],
             compiler_params=pltpu.CompilerParams(
                 collective_id=0, has_side_effects=True, vmem_limit_bytes=60 * 1024 * 1024
             ),

time: 43.4 us -> 42.4 us (0.977)
  Pallas kernels: 42.6 us -> 41.6 us
    pallas_call x1, Pallas kernels: 42.6 us -> 41.6 us  [shards(): pl.pallas_call(kernel, out_shape=pltpu.VMEM((1, ROWS, HEADS * HD), BF16),...]
where the time goes in v3:
time: 42.4 us; the launch traced here: 42.2 us
  Pallas kernels  41.6 us (98%)
  local copies, waits for them, and re-layouts  0.62 us (1%)
    pallas_call x1, Pallas kernels, shards(): pl.pallas_call(kernel, out_shape=pltpu.VMEM((1, ROWS, HEADS * HD), BF16),...  41.6 us

profile of v3, /device:TPU:1, one launch (start us, length us, event | category | flops | bytes accessed | tf_op | source)
XLA Modules:
  0.0 42.2 jit_solution(10166617360463771819)
XLA Ops:
  0.0 41.6 %shard_map.46 = bf16[1,8,2560]{2,1,0:T(8,128)(2,1)S(1)} custom-call(s32[8]{0:T(128)} %span_ref.1, bf16[1,8,2560]{2,1,0:T(8,128)(2,1)} %q_ref.1, bf16[1,8,2560]{2,1,0:T(8,128)(2,1)} %k_ref.1, bf16[1,8,2560]{2,1,0:T(8,128)(2,1)} %v_ref.1), custom_call_target="tpu_custom_call" | custom-call | tf_op jit(solution)/shard_map/pallas_call | solution.py:299
  41.6 0.6 %copy.6 = bf16[1,8,2560]{2,1,0:T(8,128)(2,1)} copy(bf16[1,8,2560]{2,1,0:T(8,128)(2,1)S(1)} %shard_map.46) | data formatting | bytes 81920

commit v4 on v3

--- a/solution.py
+++ b/solution.py
@@ -26,6 +26,17 @@
 HEAD_SEQ = tuple(y * HALF + z * 2 for z in HEAD_Z for y in range(2))
 
 
+NEAR_Z = 8
+NEAR = tuple(seq % HALF < 2 * NEAR_Z for seq in HEAD_SEQ)
+
+
+def near_of(head):
+    near = jnp.bool_(NEAR[0])
+    for h in range(1, HEADS):
+        near = jnp.where(head == h, NEAR[h], near)
+    return near
+
+
 def seq_of(head):
     if isinstance(head, int):
         return HEAD_SEQ[head]
@@ -103,12 +114,25 @@
                         def _():
                             greet((group, sender))
 
+        @pl.when(near_of(head))
+        def _():
+            for k in sorted(range(ZS), key=lambda k: -min(k, ZS - k)):
+                far = (z + k) % ZS
+                for y in range(2):
+                    for c in range(2):
+                        sender = y * HALF + 2 * far + c
+                        via = (part_of(head) + jnp.where(head < 2 * GROUPS, 0, c) + far) % GROUPS
+
+                        @pl.when(jnp.logical_or(via != group, sender != me))
+                        def _():
+                            greet((via, sender))
+
         for step in range(1, GROUPS, 2):
             greet(((group + step) % GROUPS, me))
 
     @pl.when(jnp.logical_not(is_head))
     def _():
-        for h in range(HEADS):
+        for h in sorted(range(HEADS), key=lambda h: HEAD_SEQ[h] % HALF):
             greet((group, seq_of(h)))
 
     for step in range(1, GROUPS):
@@ -135,11 +159,10 @@
 
     spans = [span[g] for g in range(GROUPS)]
     sources = []
-    for step in range(GROUPS):
-        wanted = span[(group + step) % GROUPS] - 1
+    for g in range(GROUPS):
         source = jnp.int32(0)
         for p in range(GROUPS):
-            source = jnp.where(spans[p] == wanted, p, source)
+            source = jnp.where(spans[p] == spans[g] - 1, p, source)
         sources.append(source)
     my_span = span[group]
     before = jnp.int32(0)
@@ -148,12 +171,19 @@
 
     targets = [seq_of(h) for h in part_heads(part)]
     sent = 2 * GROUPS + jnp.where(third, GROUPS, 0) - jnp.where(to_self, 1, 0)
-    greeted = GROUPS - 1 + jnp.where(is_head, SEQ - 1 + GROUPS // 2, HEADS)
+    near_targets = [near_of(h) for h in part_heads(part)]
+    near_sent = sum(jnp.where(near, GROUPS, 0) for near in near_targets[:2])
+    near_sent += jnp.where(jnp.logical_and(third, near_targets[2]), GROUPS, 0)
+    near_sent -= jnp.where(jnp.logical_and(to_self, near_of(head)), 1, 0)
+    far_heads = sum(jnp.where(near, 0, 1) for near in near_targets[:2])
+    far_heads += jnp.where(jnp.logical_and(third, jnp.logical_not(near_targets[2])), 1, 0)
+    far_heads -= jnp.where(jnp.logical_and(to_self, jnp.logical_not(near_of(head))), 1, 0)
+    greeted = near_sent + GROUPS - 1 + jnp.where(is_head, SEQ - 1 + GROUPS // 2, HEADS)
     pl.semaphore_wait(barrier, greeted)
 
     for step in (4, 3, 5, 2, 6, 1, 7):
         send("part", parts.at[(part + step) % GROUPS], inter.at[group], (part_send, part_recv), peer(step))
-    @pl.when(is_head)
+    @pl.when(jnp.logical_and(is_head, jnp.logical_not(near_of(head))))
     def _():
         for c in range(2):
             low = (group + 2 * GROUPS - part_of(head) - jnp.where(head < 2 * GROUPS, 0, c)) % GROUPS
@@ -165,11 +195,14 @@
                     def _():
                         pl.semaphore_signal(go, inc=1, device_id=(group, passer), device_id_type=MESH)
 
-    for h in range(HEADS):
-
-        @pl.when(me != seq_of(h))
-        def _(h=h):
-            send("own", pack.at[h], own.at[me], (own_send, own_recv), (group, seq_of(h)))
+    farthest = ((z + 8 + ZS - 3) % ZS * 5) // 4
+    for k in range(HEADS):
+        h = (farthest + (k + 1) // 2 * (1 if k % 2 else -1) + HEADS) % HEADS
+        target = seq_of(h)
+
+        @pl.when(me != target)
+        def _(h=h, target=target):
+            send("own", pack.at[h], own.at[me], (own_send, own_recv), (group, target))
 
     @pl.when(is_head)
     def _():
@@ -178,32 +211,29 @@
     others = inter.at[pl.ds(0, GROUPS - 1)]
     wait("part", others, part_recv)
 
-    pl.semaphore_wait(go, 2 + jnp.where(third, 1, 0) - jnp.where(to_self, 1, 0))
-
-    def pass_on(step, i):
-        def copy():
-            device = ((group + step) % GROUPS, targets[i])
-            send("prev", picked.at[step, i], prev.at[me], (prev_send, prev_recv), device)
-
-        if step:
-            copy()
-        else:
-            pl.when(me != targets[i])(copy)
-
-            @pl.when(me == targets[i])
-            def _():
-                prev[me] = picked[step, i]
-
-    order = (5, 3, 4, 7, 1, 6, 2, 0)
-    for step in order:
-        picked[step] = inter[sources[step]]
+    @pl.when(far_heads > 0)
+    def _():
+        pl.semaphore_wait(go, far_heads)
+
+    def pass_on(g, i):
+        here = jnp.logical_and(group == g, me == targets[i])
+
+        @pl.when(jnp.logical_not(here))
+        def _():
+            send("prev", picked.at[g, i], prev.at[me], (prev_send, prev_recv), (g, targets[i]))
+
+        @pl.when(here)
+        def _():
+            prev[me] = picked[g, i]
+
+    for g in (0, 4, 2, 6, 1, 5, 3, 7):
+        picked[g] = inter[sources[g]]
         for i in range(2):
-            pass_on(step, i)
-
-    @pl.when(third)
-    def _():
-        for step in order:
-            pass_on(step, 2)
+            pass_on(g, i)
+
+        @pl.when(third)
+        def _(g=g):
+            pass_on(g, 2)
 
     @pl.when(is_head)
     def _():

time: 42.4 us -> 41 us (0.967)
  Pallas kernels: 41.6 us -> 40.2 us
    pallas_call x1, Pallas kernels: 41.6 us -> 40.2 us  [shards(): pl.pallas_call(kernel, out_shape=pltpu.VMEM((1, ROWS, HEADS * HD), BF16),...]
where the time goes in v4:
time: 41 us; the launch traced here: 40.8 us
  Pallas kernels  40.2 us (98%)
  local copies, waits for them, and re-layouts  0.62 us (2%)
    pallas_call x1, Pallas kernels, shards(): pl.pallas_call(kernel, out_shape=pltpu.VMEM((1, ROWS, HEADS * HD), BF16),...  40.2 us

profile of v4, /device:TPU:1, one launch (start us, length us, event | category | flops | bytes accessed | tf_op | source)
XLA Modules:
  0.0 40.8 jit_solution(9670247654666459173)
XLA Ops:
  0.0 40.2 %shard_map.46 = bf16[1,8,2560]{2,1,0:T(8,128)(2,1)S(1)} custom-call(s32[8]{0:T(128)} %span_ref.1, bf16[1,8,2560]{2,1,0:T(8,128)(2,1)} %q_ref.1, bf16[1,8,2560]{2,1,0:T(8,128)(2,1)} %k_ref.1, bf16[1,8,2560]{2,1,0:T(8,128)(2,1)} %v_ref.1), custom_call_target="tpu_custom_call" | custom-call | tf_op jit(solution)/shard_map/pallas_call | solution.py:329
  40.2 0.6 %copy.6 = bf16[1,8,2560]{2,1,0:T(8,128)(2,1)} copy(bf16[1,8,2560]{2,1,0:T(8,128)(2,1)S(1)} %shard_map.46) | data formatting | bytes 81920

commit v5 on v4

--- a/solution.py
+++ b/solution.py
@@ -14,8 +14,7 @@
 ROWS = 8
 HALF = SEQ // 2
 ZS = HALF // 2
-CHUNK = 128
-SLOTS = CHUNK // ROWS
+BANDS = ((0, 2), (2, 2), (4, 4), (8, 8))
 MESH = pl.DeviceIdType.MESH
 F32 = jnp.float32
 BF16 = jnp.bfloat16
@@ -79,7 +78,7 @@
 
 def kernel(
     span_ref, q_ref, k_ref, v_ref, out_ref,
-    span, inbox, pack, parts, inter, picked, own, prev, stats, acc, osend, ogot,
+    span, inbox, pack, parts, inter, picked, own, prev, stats, acc, osend,
     in_sem, span_sem, part_send, part_recv, own_send, own_recv, prev_send, prev_recv, out_send, out_recv, go,
 ):
     group = lax.axis_index("span")
@@ -242,20 +241,23 @@
         keys = own[:, 1].reshape(SEQ * ROWS, HD)
         values = own[:, 2].reshape(SEQ * ROWS, HD)
 
-        def slots_of(c):
-            return [pl.ds(y * HALF + c * SLOTS // 2, SLOTS // 2) for y in range(2)]
-
-        def queries_of(c):
-            return jnp.concatenate([own[slots, 0].reshape(CHUNK // 2, HD) for slots in slots_of(c)], 0)
-
-        for c in range(SEQ // SLOTS):
-            rows = pl.ds(c * CHUNK, CHUNK)
-            queries = queries_of(c)
+        def slots_of(first, count):
+            return [pl.ds(y * HALF + 2 * first, 2 * count) for y in range(2)]
+
+        def rows_of(first, count):
+            return pl.ds(4 * ROWS * first, 4 * ROWS * count)
+
+        def queries_of(first, count):
+            return jnp.concatenate([own[slots, 0].reshape(2 * ROWS * count, HD) for slots in slots_of(first, count)], 0)
+
+        for first, count in BANDS:
+            rows = rows_of(first, count)
+            queries = queries_of(first, count)
             scores = dot(queries, keys, ((1,), (1,)))
             top = jnp.max(scores, axis=1, keepdims=True)
             weights = jnp.exp((scores - top) * SCALE)
-            stats[0, rows] = jnp.broadcast_to(top, (CHUNK, HD))
-            stats[1, rows] = jnp.broadcast_to(jnp.sum(weights, axis=1, keepdims=True), (CHUNK, HD))
+            stats[0, rows] = jnp.broadcast_to(top, (4 * ROWS * count, HD))
+            stats[1, rows] = jnp.broadcast_to(jnp.sum(weights, axis=1, keepdims=True), (4 * ROWS * count, HD))
             acc[rows] = dot(weights.astype(BF16), values, ((1,), (0,)))
 
         @pl.when(to_self)
@@ -270,9 +272,10 @@
         keys2 = prev[:, 0].reshape(SEQ * ROWS, HD)
         values2 = prev[:, 1].reshape(SEQ * ROWS, HD)
 
-        for c in range(SEQ // SLOTS):
-            rows = pl.ds(c * CHUNK, CHUNK)
-            queries = queries_of(c)
+        columns = out_ref.at[0, :, pl.ds(pl.multiple_of(head * HD, HD), HD)]
+        for first, count in BANDS:
+            rows = rows_of(first, count)
+            queries = queries_of(first, count)
             scores = dot(queries, keys2, ((1,), (1,)))
             scores = jnp.where(before > 0, scores, -1e30)
             old = stats[0, rows][:, :1]
@@ -281,29 +284,25 @@
             fade = jnp.exp((old - top) * SCALE)
             total = stats[1, rows][:, :1] * fade + jnp.sum(weights, axis=1, keepdims=True)
             result = acc[rows] * fade + dot(weights.astype(BF16), values2, ((1,), (0,)))
-            result = (result / total).reshape(2, SLOTS // 2, ROWS, HD).astype(BF16)
-            for y, slots in enumerate(slots_of(c)):
+            result = (result * (1.0 / total)).reshape(2, 2 * count, ROWS, HD).astype(BF16)
+            for y, slots in enumerate(slots_of(first, count)):
                 osend[slots] = result[y]
-            for i in range(SLOTS):
-                slot = (i % 2) * HALF + c * SLOTS // 2 + i // 2
+            for i in range(4 * count):
+                slot = i // 2 % 2 * HALF + 2 * (first + i // 4) + (i + 1) % 2
 
                 @pl.when(slot != me)
                 def _(slot=slot):
-                    send("out", osend.at[slot], ogot.at[head], (out_send, out_recv), (group, slot))
-
-        ogot[head] = osend[me]
-
-    @pl.when(is_head)
-    def _():
-        whole = ogot.at[pl.ds(0, HEADS - 1)]
-        wait("out", whole, out_recv)
+                    send("out", osend.at[slot], columns, (out_send, out_recv), (group, slot))
+
+        out_ref[0, :, pl.ds(pl.multiple_of(head * HD, HD), HD)] = osend[me]
+
+    @pl.when(is_head)
+    def _():
+        wait("out", out_ref.at[0, :, pl.ds(0, (HEADS - 1) * HD)], out_recv)
 
     @pl.when(jnp.logical_not(is_head))
     def _():
-        wait("out", ogot, out_recv)
-
-    for h in range(HEADS):
-        out_ref[0, :, h * HD : (h + 1) * HD] = ogot[h]
+        wait("out", out_ref.at[0], out_recv)
 
     wait("part", others, part_send)
 
@@ -343,7 +342,6 @@
                 pltpu.VMEM((2, SEQ * ROWS, HD), F32),
                 pltpu.VMEM((SEQ * ROWS, HD), F32),
                 pltpu.VMEM((SEQ, ROWS, HD), BF16),
-                pltpu.VMEM((HEADS, ROWS, HD), BF16),
                 pltpu.SemaphoreType.DMA((3,)),
             ]
             + [pltpu.SemaphoreType.DMA] * 9

time: 41 us -> 40.7 us (level)
  no operation moved by 1% of the time
where the time goes in v5:
time: 40.7 us; the launch traced here: 40.5 us
  Pallas kernels  39.9 us (98%)
  local copies, waits for them, and re-layouts  0.62 us (2%)
    pallas_call x1, Pallas kernels, shards(): pl.pallas_call(kernel, out_shape=pltpu.VMEM((1, ROWS, HEADS * HD), BF16),...  39.9 us

profile of v5, /device:TPU:1, one launch (start us, length us, event | category | flops | bytes accessed | tf_op | source)
XLA Modules:
  0.0 40.5 jit_solution(13673440259438190930)
XLA Ops:
  0.0 39.9 %shard_map.46 = bf16[1,8,2560]{2,1,0:T(8,128)(2,1)S(1)} custom-call(s32[8]{0:T(128)} %span_ref.1, bf16[1,8,2560]{2,1,0:T(8,128)(2,1)} %q_ref.1, bf16[1,8,2560]{2,1,0:T(8,128)(2,1)} %k_ref.1, bf16[1,8,2560]{2,1,0:T(8,128)(2,1)} %v_ref.1), custom_call_target="tpu_custom_call" | custom-call | tf_op jit(solution)/shard_map/pallas_call | solution.py:328
  39.9 0.6 %copy.6 = bf16[1,8,2560]{2,1,0:T(8,128)(2,1)} copy(bf16[1,8,2560]{2,1,0:T(8,128)(2,1)S(1)} %shard_map.46) | data formatting | bytes 81920

commit v6 on v5

--- a/solution.py
+++ b/solution.py
@@ -21,7 +21,7 @@
 SCALE = HD**-0.5
 
 
-HEAD_Z = (3, 4, 6, 8, 9, 11, 12, 14, 0, 1)
+HEAD_Z = (3, 4, 6, 7, 9, 11, 12, 14, 0, 1)
 HEAD_SEQ = tuple(y * HALF + z * 2 for z in HEAD_Z for y in range(2))
 
 
@@ -181,7 +181,18 @@
     pl.semaphore_wait(barrier, greeted)
 
     for step in (4, 3, 5, 2, 6, 1, 7):
-        send("part", parts.at[(part + step) % GROUPS], inter.at[group], (part_send, part_recv), peer(step))
+        full = third if step % 2 == 0 else jnp.logical_not(third)
+
+        @pl.when(full)
+        def _(step=step):
+            send("part", parts.at[(part + step) % GROUPS], inter.at[group], (part_send, part_recv), peer(step))
+
+        @pl.when(jnp.logical_not(full))
+        def _(step=step):
+            two = pl.ds(0, 2)
+            source, target = parts.at[(part + step) % GROUPS, two], inter.at[group, two]
+            send("part", source, target, (part_send, part_recv), peer(step))
+
     @pl.when(jnp.logical_and(is_head, jnp.logical_not(near_of(head))))
     def _():
         for c in range(2):
@@ -194,7 +205,7 @@
                     def _():
                         pl.semaphore_signal(go, inc=1, device_id=(group, passer), device_id_type=MESH)
 
-    farthest = ((z + 8 + ZS - 3) % ZS * 5) // 4
+    farthest = ((z + ZS - 3) % ZS * 5) // 4
     for k in range(HEADS):
         h = (farthest + (k + 1) // 2 * (1 if k % 2 else -1) + HEADS) % HEADS
         target = seq_of(h)
@@ -207,8 +218,13 @@
     def _():
         own[me] = pack[head]
 
-    others = inter.at[pl.ds(0, GROUPS - 1)]
-    wait("part", others, part_recv)
+    @pl.when(third)
+    def _():
+        wait("part", inter.at[pl.ds(0, GROUPS - 1)], part_recv)
+
+    @pl.when(jnp.logical_not(third))
+    def _():
+        wait("part", inter.at[pl.ds(0, GROUPS - 1), pl.ds(0, 2)], part_recv)
 
     @pl.when(far_heads > 0)
     def _():
@@ -226,12 +242,14 @@
             prev[me] = picked[g, i]
 
     for g in (0, 4, 2, 6, 1, 5, 3, 7):
-        picked[g] = inter[sources[g]]
+        picked[g, pl.ds(0, 2)] = inter[sources[g], pl.ds(0, 2)]
         for i in range(2):
             pass_on(g, i)
 
-        @pl.when(third)
-        def _(g=g):
+    @pl.when(third)
+    def _():
+        for g in (0, 4, 2, 6, 1, 5, 3, 7):
+            picked[g, 2] = inter[sources[g], 2]
             pass_on(g, 2)
 
     @pl.when(is_head)
@@ -304,7 +322,13 @@
     def _():
         wait("out", out_ref.at[0], out_recv)
 
-    wait("part", others, part_send)
+    @pl.when(third)
+    def _():
+        wait("part", prev.at[pl.ds(0, 3 * 3 + 4 * 2)], part_send)
+
+    @pl.when(jnp.logical_not(third))
+    def _():
+        wait("part", prev.at[pl.ds(0, 3 * 2 + 4 * 3)], part_send)
 
     @pl.when(is_head)
     def _():

time: 40.7 us -> 40.6 us (level)
  no operation moved by 1% of the time
where the time goes in v6:
time: 40.6 us; the launch traced here: 40.5 us
  Pallas kernels  39.8 us (98%)
  local copies, waits for them, and re-layouts  0.62 us (2%)
    pallas_call x1, Pallas kernels, shards(): pl.pallas_call(kernel, out_shape=pltpu.VMEM((1, ROWS, HEADS * HD), BF16),...  39.8 us

profile of v6, /device:TPU:1, one launch (start us, length us, event | category | flops | bytes accessed | tf_op | source)
XLA Modules:
  0.0 40.5 jit_solution(11137773535677336381)
XLA Ops:
  0.0 39.8 %shard_map.46 = bf16[1,8,2560]{2,1,0:T(8,128)(2,1)S(1)} custom-call(s32[8]{0:T(128)} %span_ref.1, bf16[1,8,2560]{2,1,0:T(8,128)(2,1)} %q_ref.1, bf16[1,8,2560]{2,1,0:T(8,128)(2,1)} %k_ref.1, bf16[1,8,2560]{2,1,0:T(8,128)(2,1)} %v_ref.1), custom_call_target="tpu_custom_call" | custom-call | tf_op jit(solution)/shard_map/pallas_call | solution.py:352
  39.8 0.6 %copy.6 = bf16[1,8,2560]{2,1,0:T(8,128)(2,1)} copy(bf16[1,8,2560]{2,1,0:T(8,128)(2,1)S(1)} %shard_map.46) | data formatting | bytes 81920

commit v7 on v5

--- a/solution.py
+++ b/solution.py
@@ -221,10 +221,6 @@
         def _():
             send("prev", picked.at[g, i], prev.at[me], (prev_send, prev_recv), (g, targets[i]))
 
-        @pl.when(here)
-        def _():
-            prev[me] = picked[g, i]
-
     for g in (0, 4, 2, 6, 1, 5, 3, 7):
         picked[g] = inter[sources[g]]
         for i in range(2):
@@ -233,6 +229,10 @@
         @pl.when(third)
         def _(g=g):
             pass_on(g, 2)
+
+    @pl.when(to_self)
+    def _():
+        prev[me] = picked[group, jnp.where(head < 2 * GROUPS, head % 2, 2)]
 
     @pl.when(is_head)
     def _():

time: 40.7 us -> 40.7 us (level)
  no operation moved by 1% of the time
where the time goes in v7:
time: 40.7 us; the launch traced here: 40.5 us
  Pallas kernels  39.9 us (98%)
  local copies, waits for them, and re-layouts  0.62 us (2%)
    pallas_call x1, Pallas kernels, shards(): pl.pallas_call(kernel, out_shape=pltpu.VMEM((1, ROWS, HEADS * HD), BF16),...  39.9 us

profile of v7, /device:TPU:1, one launch (start us, length us, event | category | flops | bytes accessed | tf_op | source)
XLA Modules:
  0.0 40.5 jit_solution(8958414480984386231)
XLA Ops:
  0.0 39.9 %shard_map.46 = bf16[1,8,2560]{2,1,0:T(8,128)(2,1)S(1)} custom-call(s32[8]{0:T(128)} %span_ref.1, bf16[1,8,2560]{2,1,0:T(8,128)(2,1)} %q_ref.1, bf16[1,8,2560]{2,1,0:T(8,128)(2,1)} %k_ref.1, bf16[1,8,2560]{2,1,0:T(8,128)(2,1)} %v_ref.1), custom_call_target="tpu_custom_call" | custom-call | tf_op jit(solution)/shard_map/pallas_call | solution.py:328
  39.9 0.6 %copy.6 = bf16[1,8,2560]{2,1,0:T(8,128)(2,1)} copy(bf16[1,8,2560]{2,1,0:T(8,128)(2,1)S(1)} %shard_map.46) | data formatting | bytes 81920
